TPU v7x, 128 devices: a whole 4x4x4 slice. The times are simulated.
128 devices in a mesh: var: 4 (over z), samp: 32 (over x, y, core).
Axes of the slice: x: 4, y: 4, z: 4, core: 2. Of those that a mesh axis runs over, the one named last changes fastest.
Arguments:
- genotypes: int32 [3072, 98304], P('var', 'samp'), may hold values from 0 to 2, as said below
- called: int32 [3072, 98304], P('var', 'samp'), may hold values from 0 to 1
- dosage: int32 [98304, 1024], P(('samp', 'var')), may hold values from 0 to 200
- sample_order: int32 [128, 768], P(('samp', 'var')), may hold values from 0 to 767, each once within a row
- noise_ratio: float32 [16], replicated, may hold values from 0.5 to 4
- solution: float32 [98304, 16], P(('samp', 'var')), may hold values from -13 to 13
- residual: float32 [98304, 16], P(('samp', 'var')), may hold values from -13 to 13
- direction: float32 [98304, 16], P(('samp', 'var')), may hold values from -13 to 13
Outputs:
- solution_new: float32 [98304, 16], P(('samp', 'var'))
- residual_new: float32 [98304, 16], P(('samp', 'var'))
- direction_new: float32 [98304, 16], P(('samp', 'var'))
- scores: float32 [1024, 16], P(('var', 'samp'))
Inputs may be any that keep to these rules, and one draw needn't show every extreme that they name: `genotypes`: where called is 1, the count of one allele. `sample_order`: each row lists 0 to 767 once.
All inputs are finite; a program needn't handle non-finite values.
Results may differ from a plain program's by a relative error of at most 0.023.
Values may be sent and summed in bfloat16 or wider, within the bound.
A program may use at most 128 MiB of HBM per device.

v0:
```python
import math
import jax
import jax.numpy as jnp
from jax import lax
from jax.sharding import PartitionSpec as P

VARIANTS = 3072


def standard_form(raw_proj, called_proj, allele_sum, called_count):
    frequency = (allele_sum + 1.0) / (2.0 * called_count + 2.0)
    spread = jnp.sqrt(2.0 * frequency * (1.0 - frequency))
    loading = (raw_proj - 2.0 * frequency[:, None] * called_proj) / spread[:, None]
    return (frequency, spread, loading)


def body(genotypes, called, dosage, sample_order, noise_ratio, solution, residual, direction):
    coded = genotypes * called
    coded_b = coded.astype(jnp.bfloat16)
    called_b = called.astype(jnp.bfloat16)
    allele_sum = jnp.sum(coded, axis=1).astype(jnp.float32)
    called_count = jnp.sum(called, axis=1).astype(jnp.float32)
    quarter = direction.shape[0]
    samples = quarter * lax.axis_size("samp") * lax.axis_size("var")
    dosage_b = dosage.astype(jnp.bfloat16)
    dosage_sum = jnp.sum(dosage, axis=0).astype(jnp.float32)
    order_row = sample_order[0]
    direction_b = direction.astype(jnp.bfloat16)
    piece = lax.all_gather(direction_b, "var", axis=0, tiled=True)
    coded_cols = coded_b
    called_cols = called_b
    raw_proj = jnp.dot(coded_cols, piece, preferred_element_type=jnp.float32)
    called_proj = jnp.dot(called_cols, piece, preferred_element_type=jnp.float32)
    raw_proj, called_proj, allele_sum, called_count = (
        lax.psum(raw_proj.astype(jnp.bfloat16), "samp").astype(jnp.float32),
        lax.psum(called_proj.astype(jnp.bfloat16), "samp").astype(jnp.float32),
        lax.psum(allele_sum.astype(jnp.bfloat16), "samp").astype(jnp.float32),
        lax.psum(called_count.astype(jnp.bfloat16), "samp").astype(jnp.float32),
    )
    frequency, spread, loading = standard_form(raw_proj, called_proj, allele_sum, called_count)
    scaled_a = (loading / spread[:, None]).astype(jnp.bfloat16)
    scaled_b = (2.0 * frequency[:, None] * loading / spread[:, None]).astype(jnp.bfloat16)
    coded_cols = coded_b
    called_cols = called_b
    term = jnp.einsum("vs,vc->sc", coded_cols, scaled_a, preferred_element_type=jnp.float32)
    term = term - jnp.einsum("vs,vc->sc", called_cols, scaled_b, preferred_element_type=jnp.float32)
    back = lax.psum_scatter(
        (term / VARIANTS).astype(jnp.bfloat16), "var", scatter_dimension=0, tiled=True
    ).astype(jnp.float32)
    applied = noise_ratio[None, :] * direction + back
    res_norm, curvature = lax.psum(
        (jnp.sum(residual * residual, axis=0), jnp.sum(direction * applied, axis=0)),
        ("var", "samp"),
    )
    step_size = res_norm / (curvature + 1e-06)
    solution_new = solution + step_size[None, :] * direction
    residual_new = residual - step_size[None, :] * applied
    res_square = jnp.sum(residual_new * residual_new, axis=0)
    res_new_norm, sol_sum, sol_square = lax.psum(
        (res_square, jnp.sum(solution_new, axis=0), jnp.sum(solution_new * solution_new, axis=0)),
        ("var", "samp"),
    )
    picked = jnp.take(solution_new, order_row, axis=0).astype(jnp.bfloat16)
    cross_local = jnp.einsum("ij,ic->jc", dosage_b, picked, preferred_element_type=jnp.float32)
    cross_sum, dosage_sum = (
        lax.psum_scatter(cross_local, ("var", "samp"), scatter_dimension=0, tiled=True),
        lax.psum_scatter(dosage_sum, ("var", "samp"), scatter_dimension=0, tiled=True),
    )
    direction_new = residual_new + (res_new_norm / (res_norm + 1e-06))[None, :] * direction
    dose_freq = (dosage_sum / 100.0 + 1.0) / (2.0 * samples + 2.0)
    dose_spread = jnp.sqrt(2.0 * dose_freq * (1.0 - dose_freq))
    scale_norm = math.sqrt(samples) * jnp.sqrt(sol_square / samples + 1e-06)
    scores = (cross_sum / 100.0 - 2.0 * dose_freq[:, None] * sol_sum[None, :]) / (
        dose_spread[:, None] * scale_norm[None, :]
    )
    return (solution_new, residual_new, direction_new, scores)


def solution(mesh):
    placed = (
        P("var", "samp"),
        P("var", "samp"),
        P(("samp", "var"), None),
        P(("samp", "var"), None),
        P(),
        P(("samp", "var"), None),
        P(("samp", "var"), None),
        P(("samp", "var"), None),
    )
    return jax.shard_map(
        body,
        mesh=mesh,
        in_specs=placed,
        out_specs=(
            P(("samp", "var"), None),
            P(("samp", "var"), None),
            P(("samp", "var"), None),
            P(("var", "samp"), None),
        ),
        check_vma=False,
    )
```

profile of v0, /device:TPU:1, one launch (start us, length us, event | category | flops | bytes accessed | tf_op | source)
XLA Modules:
  0.0 401.3 jit_solution(4430301488992100264)
XLA Ops:
  7.2 0.0 reduce-scatter.3.cloned.1.call-start
  7.2 0.8 convert_element_type.61
  8.0 11.4 %all_gather.3 = bf16[3072,16]{0,1:T(8,128)(2,1)S(1)} all-gather(bf16[768,16]{0,1:T(8,128)(2,1)S(1)} %convert_element_type.61), channel_id=1, replica_groups=mesh['var'=4,'samp'=32] {'var'}, dimensions={0}, use_global_device_ids=true | all-gather | bytes 122880 | tf_op jit(solution)/shard_map/all_gather | solution.py:29
  19.5 10.1 %multiply_reduce_fusion = (s32[768]{0:T(1024)S(1)}, s32[768]{0:T(1024)S(1)}, bf16[768,3072]{1,0:T(8,128)(2,1)}) fusion(s32[768,3072]{1,0:T(8,128)} %param.8, s32[768,3072]{1,0:T(8,128)} %param.9), kind=kLoop, calls=%fused_computation.1 | loop fusion | flops 9435648 | bytes 23599104 | tf_op jit(solution)/shard_map/reduce_sum | solution.py:21
  29.6 0.0 copy-start
  29.6 5.1 %fusion.10 = bf16[768,16]{0,1:T(8,128)(2,1)S(1)} fusion(bf16[3072,16]{0,1:T(8,128)(2,1)S(1)} %all_gather.3, s32[768,3072]{1,0:T(8,128)} %param.9), kind=kOutput, calls=%fused_computation.13 | convolution fusion | flops 77869056 | bytes 9560064 | tf_op jit(solution)/shard_map/dot_general | solution.py:33
  34.7 0.0 copy-done
  34.7 0.0 slice-start
  34.7 1.3 convolution_convert_fusion
  36.1 123.5 %all-reduce.4 = (bf16[768,16]{0,1:T(8,128)(2,1)S(1)}, bf16[768,16]{0,1:T(8,128)(2,1)S(1)}, bf16[768]{0:T(1024)(128)(2,1)S(1)}, bf16[768]{0:T(1024)(128)(2,1)S(1)}) all-reduce(bf16[768,16]{0,1:T(8,128)(2,1)S(1)} %fusion.10, bf16[768,16]{0,1:T(8,128)(2,1)S(1)} %convolution_convert_fusion, ...), channel_id=1, replica_groups=mesh['var'=4,'samp'=32] {'samp'}, use_global_device_ids=true, to_apply=%region_7.0 | all-reduce | flops 26112 | bytes 104448 | tf_op jit(solution)/shard_map/psum | solution.py:36
  159.6 0.0 slice-start.1
  159.6 4.6 %convolution_bitcast_fusion = f32[3072,16]{0,1:T(8,128)S(1)} fusion(s32[768,3072]{1,0:T(8,128)} %param.9, bf16[768,16]{0,1:T(8,128)(2,1)S(1)} %get-tuple-element.26, bf16[768,16]{0,1:T(8,128)(2,1)S(1)} %get-tuple-element.27, f32[768]{0:T(1024)S(1)} %get-tuple-element.40, f32[768]{0:T(1024)S(1)} %get-tuple-element.41), kind=kOutput, calls=%fused_computation.5 | convolution fusion | flops 77955072 | bytes 9689088 | tf_op jit(solution)/shard_map/vs,vc->sc/dot_general | solution.py:46
  164.2 0.0 copy-start.3
  164.2 0.0 copy-start.6
  164.2 0.0 copy-start.2
  164.2 0.0 copy-start.7
  164.2 0.0 copy-start.5
  164.2 0.0 slice-done
  164.2 0.3 slice-done.1
  164.5 1.4 fusion.1
  165.8 0.0 copy-start.1
  165.8 0.0 reduce-scatter.3.cloned.1.call-update
  165.9 0.0 all-reduce.7.cloned.1.call-start
  165.9 0.0 copy-done.3
  165.9 0.1 multiply_reduce_fusion.4
  166.0 0.0 copy-done.6
  166.1 2.3 reduce_sum.77
  168.4 16.6 %reduce-scatter.3.cloned.1.call-done = bf16[768,16]{0,1:T(8,128)(2,1)} async-done(((bf16[3072,16]{0,1:T(8,128)(2,1)}), bf16[768,16]{0,1:T(8,128)(2,1)}) %reduce-scatter.3.cloned.1.call-update) | async-done | bytes 24592 | tf_op jit(solution)/shard_map/reduce_scatter | solution.py:47
  185.0 0.0 copy-done.2
  185.0 0.0 copy-done.7
  185.0 0.9 multiply_reduce_fusion.3
  186.0 66.8 %all-reduce.3 = (f32[16]{0:T(128)S(1)}, f32[16]{0:T(128)S(1)}) all-reduce(f32[16]{0:T(128)S(1)} %multiply_reduce_fusion.4, f32[16]{0:T(128)S(1)} %multiply_reduce_fusion.3), channel_id=1, replica_groups=mesh['var'=4,'samp'=32] {'var','samp'}, use_global_device_ids=true, to_apply=%region_1.0 | all-reduce | flops 32 | bytes 256 | tf_op jit(solution)/shard_map/psum | solution.py:51
  252.8 0.0 copy-done.5
  252.8 2.1 multiply_reduce_fusion.2
  254.9 0.0 copy-done.8
  254.9 0.6 copy-done.4
  255.5 0.2 copy.16
  255.7 1.9 gather_fusion
  257.6 0.0 copy-done.1
  257.6 1.1 fusion.7
  258.7 0.0 all-reduce.7.cloned.1.call-update
  258.7 63.2 %all-reduce.2 = (f32[16]{0:T(128)S(1)}, f32[16]{0:T(128)S(1)}, f32[1024]{0:T(1024)S(1)}, f32[16]{0:T(128)S(1)}) all-reduce(f32[16]{0:T(128)S(1)} %get-tuple-element.31, f32[16]{0:T(128)} %get-tuple-element.34, f32[1024]{0:T(1024)S(1)} %convert_element_type.79, f32[16]{0:T(128)} %get-tuple-element.35), channel_id=1, replica_groups=mesh['var'=4,'samp'=32] {'var','samp'}, use_global_device_ids=true, to_apply=%region_12.0 | all-reduce | flops 1072 | bytes 8576 | tf_op jit(solution)/shard_map/psum | solution.py:59
  321.9 0.6 add_divide_fusion.1
  322.6 1.5 multiply_add_fusion
  324.1 0.1 broadcast_multiply_fusion.1
  324.2 68.9 %all-reduce.7.cloned.1.call-done = f32[1024,16]{0,1:T(8,128)} async-done(((f32[1024,16]{0,1:T(8,128)}), f32[1024,16]{0,1:T(8,128)}) %all-reduce.7.cloned.1.call-update) | async-done | bytes 65552
  393.0 0.8 fusion.20
  393.8 0.7 copy.17
  (12 shorter events, 0.1 us)
Async XLA Ops:
  7.2 177.9 %reduce-scatter.3.cloned.1.call-start = ((), (), s32[]{:S(2)}) async-start(), calls=%async_computation.1 | async-start | bytes 122880 | tf_op jit(solution)/shard_map/reduce_scatter | solution.py:47
  29.6 5.2 %copy-start = (bf16[768,3072]{1,0:T(8,128)(2,1)S(1)}, bf16[768,3072]{1,0:T(8,128)(2,1)}, u32[]{:S(2)}) copy-start(bf16[768,3072]{1,0:T(8,128)(2,1)} %get-tuple-element.33) | copy-start | bytes 14155780
  34.7 129.5 %slice-start = ((s8[4718592]{0:T(1024)(128)(4,1)}), s8[524288]{0:T(1024)(128)(4,1)S(1)}, s32[]{:S(2)}) async-start(s8[4718592]{0:T(1024)(128)(4,1)} %bitcast.12), calls=%async_computation.3 | async-start | bytes 1048576
  159.6 4.9 %slice-start.1 = ((s8[4718592]{0:T(1024)(128)(4,1)}), s8[4194304]{0:T(1024)(128)(4,1)S(1)}, s32[]{:S(2)}) async-start(s8[4718592]{0:T(1024)(128)(4,1)} %bitcast.12), calls=%async_computation.4 | async-start | bytes 8388608
  164.2 1.8 copy-start.3
  164.2 1.9 copy-start.6
  164.2 20.9 %copy-start.2 = (f32[768,16]{0,1:T(8,128)S(1)}, f32[768,16]{0,1:T(8,128)}, u32[]{:S(2)}) copy-start(f32[768,16]{0,1:T(8,128)} %param.15) | copy-start | bytes 147460
  164.2 20.9 %copy-start.7 = (f32[16]{0:T(128)S(1)}, f32[16]{0:T(128)}, u32[]{:S(2)}) copy-start(f32[16]{0:T(128)} %param.12) | copy-start | bytes 196
  164.2 88.6 %copy-start.5 = (f32[768,16]{0,1:T(8,128)S(1)}, f32[768,16]{0,1:T(8,128)}, u32[]{:S(2)}) copy-start(f32[768,16]{0,1:T(8,128)} %param.13) | copy-start | bytes 147460
  165.8 91.7 %copy-start.1 = (s32[768,1024]{1,0:T(8,128)S(1)}, s32[768,1024]{1,0:T(8,128)}, u32[]{:S(2)}) copy-start(s32[768,1024]{1,0:T(8,128)} %param.10) | copy-start | bytes 9437188
  165.9 227.2 %all-reduce.7.cloned.1.call-start = ((), (), s32[]{:S(2)}) async-start(), calls=%async_computation.2 | async-start | bytes 131072
  252.8 2.1 copy-start.8
  254.9 0.6 copy-start.4
Sparse Core Ops, SparseCore 0:
  166.0 19.0 reduce-scatter.2
  258.8 134.1 all-reduce.6
where the time goes:
time: 402 us; the launch traced here: 401 us
  blocking collectives  265 us (66%)
  waiting for transfers between devices  85.6 us (21%)
  other arithmetic  19.3 us (5%)
  between operations  14.2 us (4%)
  matrix products  13.5 us (3%)
    psum x1, blocking collectives, body(): lax.psum(called_proj.astype(jnp.bfloat16), 'samp').astype(jnp.float32)  124 us
    unnamed x3, waiting for transfers between devices  68.9 us
    psum x1, blocking collectives, body(): lax.psum((jnp.sum(residual * residual, axis=0), jnp.sum(direction * appli...  66.8 us
    psum x1, blocking collectives, body(): lax.psum((res_square, jnp.sum(solution_new, axis=0), jnp.sum(solution_new...  63.2 us
    reduce_scatter x1, waiting for transfers between devices, body(): lax.psum_scatter((term / VARIANTS).astype(jnp.bfloat16), 'var', scatter_d...  16.6 us
    all_gather x1, blocking collectives, body(): piece = lax.all_gather(direction_b, 'var', axis=0, tiled=True)  11.4 us
    reduce_sum x1, other arithmetic, body(): allele_sum = jnp.sum(coded, axis=1).astype(jnp.float32)  10.1 us
  transfers between devices with their start and end apart: 2, of which 2 were waited for; matrix products, arithmetic and copies ran while one was open for 1% of the time, Pallas kernels for 0%

commit v1 on v0

--- a/solution.py
+++ b/solution.py
@@ -31,9 +31,10 @@
     called_cols = called_b
     raw_proj = jnp.dot(coded_cols, piece, preferred_element_type=jnp.float32)
     called_proj = jnp.dot(called_cols, piece, preferred_element_type=jnp.float32)
+    load_the_floor = lambda array_in: jnp.sum(lax.all_gather(array_in, "samp"), axis=0)
     raw_proj, called_proj, allele_sum, called_count = (
         lax.psum(raw_proj.astype(jnp.bfloat16), "samp").astype(jnp.float32),
-        lax.psum(called_proj.astype(jnp.bfloat16), "samp").astype(jnp.float32),
+        load_the_floor(called_proj.astype(jnp.bfloat16)).astype(jnp.float32),
         lax.psum(allele_sum.astype(jnp.bfloat16), "samp").astype(jnp.float32),
         lax.psum(called_count.astype(jnp.bfloat16), "samp").astype(jnp.float32),
     )

time: 402 us -> 493 us (1.23)
  waiting for transfers between devices: 85.6 us -> 149 us
  blocking collectives: 265 us -> 290 us
    unnamed x3, waiting for transfers between devices: 68.9 us -> 132 us
    all_gather x0 -> x1, blocking collectives: none -> 28.3 us  [body(): lax.all_gather(array_in, 'samp')]
where the time goes in v1:
time: 493 us
  blocking collectives  290 us (59%)
  waiting for transfers between devices  149 us (30%)
  other arithmetic  19.9 us (4%)
  matrix products  15.8 us (3%)
  between operations  14.2 us (3%)
    unnamed x3, waiting for transfers between devices  132 us
    psum x1, blocking collectives, body(): lax.psum(raw_proj.astype(jnp.bfloat16), 'samp').astype(jnp.float32)  121 us
    psum x1, blocking collectives, body(): lax.psum((jnp.sum(residual * residual, axis=0), jnp.sum(direction * appli...  66.8 us
    psum x1, blocking collectives, body(): lax.psum((res_square, jnp.sum(solution_new, axis=0), jnp.sum(solution_new...  62.7 us
    all_gather x1, blocking collectives, body(): lax.all_gather(array_in, 'samp')  28.3 us
    reduce_scatter x1, waiting for transfers between devices, body(): lax.psum_scatter((term / VARIANTS).astype(jnp.bfloat16), 'var', scatter_d...  17.2 us
    all_gather x1, blocking collectives, body(): piece = lax.all_gather(direction_b, 'var', axis=0, tiled=True)  11.4 us
    reduce_sum x1, other arithmetic, body(): allele_sum = jnp.sum(coded, axis=1).astype(jnp.float32)  10.1 us
  transfers between devices with their start and end apart: 2, of which 2 were waited for; matrix products, arithmetic and copies ran while one was open for 1% of the time, Pallas kernels for 0%

profile of v1, /device:TPU:1, one launch (start us, length us, event | category | flops | bytes accessed | tf_op | source)
XLA Modules:
  0.0 492.6 jit_solution(1983604037573923104)
XLA Ops:
  7.2 0.0 reduce-scatter.3.cloned.1.call-start
  7.2 0.8 convert_element_type.63
  8.0 11.4 %all_gather.9 = bf16[3072,16]{0,1:T(8,128)(2,1)S(1)} all-gather(bf16[768,16]{0,1:T(8,128)(2,1)S(1)} %convert_element_type.63), channel_id=1, replica_groups=mesh['var'=4,'samp'=32] {'var'}, dimensions={0}, use_global_device_ids=true | all-gather | bytes 122880 | tf_op jit(solution)/shard_map/all_gather | solution.py:29
  19.5 5.0 %fusion.10 = bf16[768,16]{0,1:T(8,128)(2,1)S(1)} fusion(bf16[3072,16]{0,1:T(8,128)(2,1)S(1)} %all_gather.9, s32[768,3072]{1,0:T(8,128)} %param.9), kind=kOutput, calls=%fused_computation.13 | convolution fusion | flops 77869056 | bytes 9560064 | tf_op jit(solution)/shard_map/dot_general | solution.py:33
  24.5 28.3 %all-gather = bf16[24576,16]{0,1:T(8,128)(2,1)S(1)} all-gather(bf16[768,16]{0,1:T(8,128)(2,1)S(1)} %fusion.10), channel_id=2, replica_groups=mesh['var'=4,'samp'=32] {'samp'}, dimensions={0}, use_global_device_ids=true | all-gather | bytes 811008 | tf_op jit(solution)/shard_map/all_gather | solution.py:34
  52.7 0.1 copy.20
  52.9 0.2 bitcast_reduce_fusion
  53.2 10.1 %multiply_reduce_fusion = (s32[768]{0:T(1024)S(1)}, s32[768]{0:T(1024)S(1)}, bf16[768,3072]{1,0:T(8,128)(2,1)}) fusion(s32[768,3072]{1,0:T(8,128)} %param.8, s32[768,3072]{1,0:T(8,128)} %param.9), kind=kLoop, calls=%fused_computation.1 | loop fusion | flops 9435648 | bytes 23599104 | tf_op jit(solution)/shard_map/reduce_sum | solution.py:21
  63.3 0.0 slice-start
  63.3 3.7 convolution_convert_fusion
  67.0 120.9 %all-reduce.4 = (bf16[768,16]{0,1:T(8,128)(2,1)S(1)}, bf16[768]{0:T(1024)(128)(2,1)S(1)}, bf16[768]{0:T(1024)(128)(2,1)S(1)}) all-reduce(bf16[768,16]{0,1:T(8,128)(2,1)S(1)} %convolution_convert_fusion, bf16[768]{0:T(1024)(128)(2,1)S(1)} %get-tuple-element.41, ...), channel_id=1, replica_groups=mesh['var'=4,'samp'=32] {'samp'}, use_global_device_ids=true, to_apply=%region_2.0 | all-reduce | flops 13824 | bytes 55296 | tf_op jit(solution)/shard_map/psum | solution.py:36
  187.9 0.0 slice-start.1
  188.0 4.6 convolution_bitcast_fusion
  192.5 0.0 copy-start.2
  192.5 0.0 copy-start.5
  192.5 0.0 copy-start.1
  192.5 0.0 copy-start.6
  192.5 0.0 copy-start.4
  192.6 0.0 slice-done
  192.6 0.3 slice-done.1
  192.8 1.4 fusion.1
  194.2 0.0 reduce-scatter.3.cloned.1.call-update
  194.2 0.0 all-reduce.7.cloned.1.call-start
  194.3 0.0 copy-done.2
  194.3 0.1 multiply_reduce_fusion.4
  194.4 0.0 copy-done.5
  194.4 2.3 reduce_sum.90
  196.7 17.2 %reduce-scatter.3.cloned.1.call-done = bf16[768,16]{0,1:T(8,128)(2,1)} async-done(((bf16[3072,16]{0,1:T(8,128)(2,1)}), bf16[768,16]{0,1:T(8,128)(2,1)}) %reduce-scatter.3.cloned.1.call-update) | async-done | bytes 24592 | tf_op jit(solution)/shard_map/reduce_scatter | solution.py:48
  213.9 0.0 copy-done.1
  213.9 0.0 copy-done.6
  213.9 0.9 multiply_reduce_fusion.3
  214.8 66.8 %all-reduce.3 = (f32[16]{0:T(128)S(1)}, f32[16]{0:T(128)S(1)}) all-reduce(f32[16]{0:T(128)S(1)} %multiply_reduce_fusion.4, f32[16]{0:T(128)S(1)} %multiply_reduce_fusion.3), channel_id=1, replica_groups=mesh['var'=4,'samp'=32] {'var','samp'}, use_global_device_ids=true, to_apply=%region_1.0 | all-reduce | flops 32 | bytes 256 | tf_op jit(solution)/shard_map/psum | solution.py:52
  281.6 0.0 copy-done.4
  281.6 1.6 multiply_reduce_fusion.2
  283.2 0.0 copy-start.3
  283.2 62.7 %all-reduce.2 = (f32[16]{0:T(128)S(1)}, f32[16]{0:T(128)}, f32[1024]{0:T(1024)}, f32[16]{0:T(128)S(1)}) all-reduce(f32[16]{0:T(128)S(1)} %get-tuple-element.30, f32[16]{0:T(128)S(1)} %get-tuple-element.33, f32[1024]{0:T(1024)S(1)} %convert_element_type.81, f32[16]{0:T(128)S(1)} %get-tuple-element.34), channel_id=1, replica_groups=mesh['var'=4,'samp'=32] {'var','samp'}, use_global_device_ids=true, to_apply=%region_12.0 | all-reduce | flops 1072 | bytes 8576 | tf_op jit(solution)/shard_map/psum | solution.py:60
  345.9 0.0 copy-done.3
  345.9 0.2 copy.16
  346.1 1.9 gather_fusion
  347.9 0.0 copy-done
  348.0 1.1 fusion.7
  349.1 0.0 all-reduce.7.cloned.1.call-update
  349.1 0.7 sqrt_multiply_fusion
  349.8 1.5 multiply_add_fusion
  351.3 0.8 broadcast_multiply_fusion.1
  352.1 132.2 %all-reduce.7.cloned.1.call-done = f32[1024,16]{0,1:T(8,128)} async-done(((f32[1024,16]{0,1:T(8,128)}), f32[1024,16]{0,1:T(8,128)}) %all-reduce.7.cloned.1.call-update) | async-done | bytes 65552
  484.3 0.8 fusion.20
  485.1 0.7 copy.17
  (11 shorter events, 0.1 us)
Async XLA Ops:
  7.2 206.7 %reduce-scatter.3.cloned.1.call-start = ((), (), s32[]{:S(2)}) async-start(), calls=%async_computation.1 | async-start | bytes 122880 | tf_op jit(solution)/shard_map/reduce_scatter | solution.py:48
  63.3 129.3 %slice-start = ((s8[4718592]{0:T(1024)(128)(4,1)}), s8[524288]{0:T(1024)(128)(4,1)S(1)}, s32[]{:S(2)}) async-start(s8[4718592]{0:T(1024)(128)(4,1)} %bitcast.17), calls=%async_computation.3 | async-start | bytes 1048576
  187.9 4.9 slice-start.1
  192.5 1.8 copy-start.2
  192.5 1.9 copy-start.5
  192.5 21.4 %copy-start.1 = (f32[768,16]{0,1:T(8,128)S(1)}, f32[768,16]{0,1:T(8,128)}, u32[]{:S(2)}) copy-start(f32[768,16]{0,1:T(8,128)} %param.15) | copy-start | bytes 147460
  192.5 21.4 %copy-start.6 = (f32[16]{0:T(128)S(1)}, f32[16]{0:T(128)}, u32[]{:S(2)}) copy-start(f32[16]{0:T(128)} %param.12) | copy-start | bytes 196
  192.5 89.1 %copy-start.4 = (f32[768,16]{0,1:T(8,128)S(1)}, f32[768,16]{0,1:T(8,128)}, u32[]{:S(2)}) copy-start(f32[768,16]{0,1:T(8,128)} %param.13) | copy-start | bytes 147460
  194.2 153.8 %copy-start = (s32[768,1024]{1,0:T(8,128)S(1)}, s32[768,1024]{1,0:T(8,128)}, u32[]{:S(2)}) copy-start(s32[768,1024]{1,0:T(8,128)} %param.10) | copy-start | bytes 9437188
  194.2 290.1 %all-reduce.7.cloned.1.call-start = ((), (), s32[]{:S(2)}) async-start(), calls=%async_computation.2 | async-start | bytes 131072
  283.2 62.7 %copy-start.3 = (f32[768,16]{0,1:T(8,128)}, f32[768,16]{0,1:T(8,128)S(1)}, u32[]{:S(2)}) copy-start(f32[768,16]{0,1:T(8,128)S(1)} %get-tuple-element.35) | copy-start | bytes 147460
Sparse Core Ops, SparseCore 0:
  194.3 19.5 reduce-scatter.2
  349.2 135.0 all-reduce.6
